TPU v7x, 512 devices: a whole 4x4x16 slice. The times are simulated.
512 devices in a mesh: segment: 2 (over core), band: 64 (over x, z_hi, y), chan: 4 (over z_lo).
Axes of the slice: x: 4, y: 4, z: 16 (z_hi: 4, z_lo: 4; z = z_hi * 4 + z_lo), core: 2. Of those that a mesh axis runs over, the one named last changes fastest.
Arguments:
- hidden_states: bfloat16 [4, 64, 64, 5120], P('segment', 'band', None, 'chan')
- modulation_shift: float32 [5120], P('chan'), may hold values from -3 to 3
- modulation_scale: float32 [5120], P('chan'), may hold values from -2.5 to 2.5
- head_weight: bfloat16 [5120, 64], P('chan'), may hold values from -0.078125 to 0.078125
- entry_weight: bfloat16 [3, 3, 3, 384, 16], P(None, None, None, 'chan')
- first_weight: bfloat16 [3, 3, 3, 384, 384], P(None, None, None, 'chan')
- first_gain: float32 [384], P('chan'), may hold values from 0.25 to 1.75
- second_weight: bfloat16 [3, 3, 3, 384, 384], P(None, None, None, 'chan'), may hold values from -0.0625 to 0.0625
- second_gain: float32 [384], P('chan'), may hold values from 0.25 to 1.75
Outputs:
- decoded: bfloat16 [384, 4, 128, 128], P('chan', 'segment', 'band')
All inputs are finite; a program needn't handle non-finite values.
Results may differ from a plain program's by a relative error of at most 0.0075.
Values may be sent and summed in bfloat16 or wider, within the bound.
A program may use at most 128 MiB of HBM per device.

v0:
```python
import jax
import jax.numpy as jnp
from jax import lax
from jax.experimental import pallas as pl
from jax.experimental.pallas import tpu as pltpu
from jax.sharding import PartitionSpec as P

D = 5120
C = 384
EPS = 1e-6
OWN = 96
X = 128
MESH = pl.DeviceIdType.MESH
NT = (((1,), (1,)), ((), ()))
F32 = jnp.float32
BF16 = jnp.bfloat16


def iota(shape, axis):
    return lax.broadcasted_iota(jnp.int32, shape, axis)


def column(row, rows):
    eye = iota((rows, X), 0) == iota((rows, X), 1)
    return jnp.sum(jnp.where(eye, jnp.broadcast_to(row, (rows, X)), 0.0), axis=1, keepdims=True)


def as_row(col):
    rows = col.shape[0]
    eye = iota((rows, X), 0) == iota((rows, X), 1)
    return jnp.sum(jnp.where(eye, jnp.broadcast_to(col, (rows, X)), 0.0), axis=0, keepdims=True)


def silu_norm(values, gain):
    power = jnp.sum(values * values, axis=0, keepdims=True) / C
    scaled = values * lax.rsqrt(power + EPS) * gain
    return (scaled * (0.5 * jnp.tanh(0.5 * scaled) + 0.5)).astype(BF16)


def kernel(
    h_ref, shift_ref, scale_ref, wt_ref, ew_ref, w1_hbm, g1_ref, w2_hbm, g2_ref,
    out_ref,
    w1, w2, parts, ewg, ewp, lat, cols, act1, raw, act2, total, gains, resid, fin,
    wsem, s_p, r_p, s_e, r_e, s_es, r_es, s_l, r_l, s_g, r_g, s_o, r_o, s_h, r_h, s_s, r_s, s_f, r_f,
):
    s, b, c = lax.axis_index("segment"), lax.axis_index("band"), lax.axis_index("chan")
    bands = lax.axis_size("band")
    up, down = lax.rem(b + 1, bands), lax.rem(b + bands - 1, bands)
    zpeers = [(s, b, lax.rem(c + d, 4)) for d in (1, 2, 3)]
    sibling = (1 - s, b, c)
    outer = (1 - s, jnp.where(s == 0, down, up), c)
    far = [(s, up, c), (1 - s, up, c), (s, down, c), (1 - s, down, c)]

    barrier = pltpu.get_barrier_semaphore()
    for peer in zpeers + [sibling] + far:
        pl.semaphore_signal(barrier, inc=1, device_id=peer, device_id_type=MESH)
    load1 = pltpu.make_async_copy(w1_hbm, w1, wsem.at[0])
    load2 = pltpu.make_async_copy(w2_hbm, w2, wsem.at[1])
    load1.start()
    load2.start()

    def remote(src, dst, send, recv, peer):
        copy = pltpu.make_async_remote_copy(
            src_ref=src, dst_ref=dst, send_sem=send, recv_sem=recv, device_id=peer, device_id_type=MESH
        )
        copy.start()
        return copy

    sent = []

    order = iota((64, 64), 0)
    source = 4 * lax.rem(order, 16) + 2 * lax.rem(order // 16, 2) + order // 32
    permute = (iota((64, 64), 1) == source).astype(F32).astype(BF16)
    weight = jnp.dot(permute, wt_ref[...], preferred_element_type=F32)
    raised = weight * (1.0 + scale_ref[...])
    high = raised.astype(BF16)
    low = (raised - high.astype(F32)).astype(BF16)
    both = lax.dot_general(jnp.concatenate([high, low], axis=0), h_ref[...], NT, preferred_element_type=F32)
    states = h_ref[...].astype(F32)
    parts[c] = jnp.zeros((72, X), F32)
    parts[c, 0:64, :] = both[0:64] + both[64:128]
    parts[c, 64:65, :] = as_row(jnp.sum(states, axis=1, keepdims=True))
    parts[c, 65:66, :] = as_row(jnp.sum(states * states, axis=1, keepdims=True))
    parts[c, 66:67, :] = as_row(jnp.sum(high.astype(F32) + low.astype(F32), axis=1, keepdims=True))
    parts[c, 67:68, :] = as_row(jnp.sum(weight * shift_ref[...], axis=1, keepdims=True))
    parts[c, 68:69, 0:OWN] = g1_ref[...]
    parts[c, 69:70, 0:OWN] = g2_ref[...]

    pl.semaphore_wait(barrier, 8)
    first = [remote(parts.at[c], parts.at[c], s_p.at[d], r_p.at[d], zpeers[d]) for d in range(3)]
    sent += first

    own_rows = pl.ds(pl.multiple_of(c * OWN, OWN), OWN)
    ewp[0:432, :] = ew_ref[...]
    ewp[432:512, :] = jnp.zeros((80, OWN), BF16)
    eye96 = (iota((OWN, OWN), 0) == iota((OWN, OWN), 1)).astype(F32).astype(BF16)
    half = ewp[pl.ds(pl.multiple_of(s * 256, 256), 256), :]
    ewg[s, own_rows, :] = lax.dot_general(eye96, half, NT, preferred_element_type=F32).astype(BF16)
    gather_e = [
        remote(ewg.at[s, own_rows], ewg.at[s, own_rows], s_e.at[d], r_e.at[d], zpeers[d]) for d in range(3)
    ]
    sent += gather_e

    zero = jnp.zeros((16, X), BF16)
    for e in range(3):
        for f in range(4):
            at = (e * 4 + f) * X
            cols[432:512, at : at + X] = jnp.zeros((80, X), BF16)
            for p in range(2 - f):
                for qr in range(9):
                    k = (p * 9 + qr) * 16
                    cols[k : k + 16, at : at + X] = zero
        act1[e, :, 0:X] = jnp.zeros((C, X), BF16)
        act2[e, :, 0:X] = jnp.zeros((C, X), BF16)

    for copy in first:
        copy.wait_recv()
    summed = (parts[0] + parts[1]) + (parts[2] + parts[3])
    center = summed[64:65] / D
    spread = summed[65:66] / D - center * center
    head = (summed[0:64] - column(summed[66:67], 64) * center) * lax.rsqrt(spread + EPS) + column(
        summed[67:68], 64
    )
    head = head.astype(BF16)
    even = lax.rem(iota((32, X), 1), 2) == 0
    for t in range(2):
        spreadout = (iota((X, X), 0) == t * 64 + iota((X, X), 1) // 2).astype(F32).astype(BF16)
        wide = jnp.dot(head, spreadout, preferred_element_type=F32)
        lat[1, 2 * s + t] = jnp.where(even, wide[0:32], wide[32:64]).astype(BF16)
    mine = pl.ds(2 * s, 2)
    latents = [remote(lat.at[1, mine], lat.at[1, mine], s_l.at[0], r_l.at[0], sibling)]
    for j, peer in enumerate(far):
        latents.append(
            remote(lat.at[1, mine], lat.at[0 if j < 2 else 2, mine], s_l.at[1 + j], r_l.at[1 + j], peer)
        )
    sent += latents
    for chan in range(4):
        for g in range(2):
            row = parts[chan, 68 + g : 69 + g, :]
            gains[g, chan * OWN : (chan + 1) * OWN, :] = jnp.broadcast_to(column(row, OWN), (OWN, X))

    for copy in gather_e:
        copy.wait_recv()
    share = remote(ewg.at[s], ewg.at[s], s_es, r_es, sibling)
    sent.append(share)
    for copy in latents:
        copy.wait_recv()

    @pl.when(b == 0)
    def _():
        lat[0] = jnp.zeros((4, 32, X), BF16)

    @pl.when(b == bands - 1)
    def _():
        lat[2] = jnp.zeros((4, 32, X), BF16)

    lane = iota((16, X), 1)
    for k in range(5):
        slot, a = (s + k) // 2, lax.rem(s + k, 2)
        for f in range(4):
            tile = lat[slot, f, pl.ds(pl.multiple_of(a * 16, 16), 16), :]
            wide = tile.astype(F32)
            shifted = [
                jnp.where(lane == 0, 0.0, pltpu.roll(wide, 1, 1)).astype(BF16),
                tile,
                jnp.where(lane == X - 1, 0.0, pltpu.roll(wide, X - 1, 1)).astype(BF16),
            ]
            for p in range(3):
                for q in range(3):
                    e, g = k - q, f + 2 - p
                    if 0 <= e < 3 and g < 4:
                        for r in range(3):
                            row = ((p * 3 + q) * 3 + r) * 16
                            at = (e * 4 + g) * X
                            cols[row : row + 16, at : at + X] = shifted[r]

    share.wait_recv()
    row_at = 2 * b + s
    for e in range(3):
        for pair in range(2):
            at = (e * 4 + pair * 2) * X
            value = jnp.dot(ewg[0], cols[0:256, at : at + 2 * X], preferred_element_type=F32)
            value += jnp.dot(ewg[1], cols[256:512, at : at + 2 * X], preferred_element_type=F32)
            rounded = value.astype(BF16)
            if e == 1:
                total[0, :, 0 : 2 * X] = rounded.astype(F32)
                resid[:, pair * 2 * X : (pair + 1) * 2 * X] = total[0, own_rows, 0 : 2 * X]
            valid = (row_at + e - 1 >= 0) & (row_at + e - 1 < 2 * bands)
            for t in range(2):
                done = silu_norm(rounded[:, t * X : (t + 1) * X].astype(F32), gains[0])
                lanes = (pair * 2 + t + 1) * X
                act1[e, :, lanes : lanes + X] = jnp.where(valid, done, jnp.zeros_like(done))

    def taps(weights, acts, q, pair):
        value = None
        for p in range(1 if pair == 0 else 0, 3):
            lanes = (pair * 2 + p - 1) * X
            rows = pl.ds(pl.multiple_of((p * 3 + q) * 288, 288), 288)
            term = jnp.dot(weights[rows, :], acts[q, :, lanes : lanes + 2 * X], preferred_element_type=F32)
            value = term if value is None else value + term
        return value

    lane96 = iota((OWN, X), 1)

    def join(value, t):
        lanes = slice(t * X, (t + 1) * X)
        left = jnp.where(lane96 == 0, 0.0, pltpu.roll(value[0:OWN, lanes], 1, 1))
        right = jnp.where(lane96 == X - 1, 0.0, pltpu.roll(value[2 * OWN : 3 * OWN, lanes], X - 1, 1))
        return left + value[OWN : 2 * OWN, lanes] + right

    near, away = 2 - 2 * s, 2 * s
    load1.wait()
    own_gather, across = [], []
    for pair in range(2):
        value = taps(w1, act1, 0, pair) + taps(w1, act1, 1, pair) + taps(w1, act1, 2, pair)
        for t in range(2):
            f = pair * 2 + t
            raw[1, f, own_rows, :] = join(value, t).astype(BF16)
            tile = raw.at[1, f, own_rows]
            across.append(remote(tile, raw.at[near, f, own_rows], s_o.at[f], r_o.at[f], outer))
            own_gather.append(
                [remote(tile, tile, s_g.at[f, d], r_g.at[f, d], zpeers[d]) for d in range(3)]
            )

    def activate(slot, f, valid):
        done = silu_norm(raw[slot, f].astype(F32), gains[1])
        lanes = (f + 1) * X
        act2[slot, :, lanes : lanes + X] = jnp.where(valid, done, jnp.zeros_like(done))

    halo, to_sibling = [], []
    for f in range(4):
        for copy in own_gather[f]:
            copy.wait_recv()
        to_sibling.append(remote(raw.at[1, f], raw.at[away, f], s_s.at[f], r_s.at[f], sibling))
        across[f].wait_recv()
        tile = raw.at[away, f, own_rows]
        halo.append([remote(tile, tile, s_h.at[f, d], r_h.at[f, d], zpeers[d]) for d in range(3)])
        activate(1, f, True)
    load2.wait()
    for pair in range(2):
        total[pair, 0:288, 0 : 2 * X] = taps(w2, act2, 1, pair)
    for f in range(4):
        to_sibling[f].wait_recv()
        activate(near, f, True)
    for pair in range(2):
        total[pair, 0:288, 0 : 2 * X] += taps(w2, act2, near, pair)
    inside = jnp.where(s == 0, b > 0, b < bands - 1)
    finals = []
    for pair in range(2):
        for f in (2 * pair, 2 * pair + 1):
            for copy in halo[f]:
                copy.wait_recv()
            activate(away, f, inside)
        value = total[pair, 0:288, 0 : 2 * X] + taps(w2, act2, away, pair)
        for t in range(2):
            f = pair * 2 + t
            decoded = (resid[:, f * X : (f + 1) * X] + join(value, t)).astype(BF16)
            fin[0, f] = decoded
    sections = remote(
        fin.at[0, pl.ds(2 * (1 - s), 2)], fin.at[1, pl.ds(2 * (1 - s), 2)], s_f, r_f, sibling
    )
    sent.append(sections)
    for t in range(2):
        out_ref[t, s] = fin[0, 2 * s + t]
    sections.wait_recv()
    for t in range(2):
        out_ref[t, 1 - s] = fin[1, 2 * s + t]
    for group in own_gather + halo:
        sent += group
    for copy in sent + across + to_sibling:
        copy.wait_send()


def body(
    hidden_states, modulation_shift, modulation_scale, head_weight, entry_weight,
    first_weight, first_gain, second_weight, second_gain,
):
    vmem = pl.BlockSpec(memory_space=pltpu.VMEM)
    anywhere = pl.BlockSpec(memory_space=pl.ANY)
    dma = pltpu.SemaphoreType.DMA
    out = pl.pallas_call(
        kernel,
        out_shape=jax.ShapeDtypeStruct((2, 2, OWN, X), BF16),
        in_specs=[vmem] * 5 + [anywhere, vmem, anywhere, vmem],
        out_specs=vmem,
        scratch_shapes=[
            pltpu.VMEM((2592, C), BF16),
            pltpu.VMEM((2592, C), BF16),
            pltpu.VMEM((4, 72, X), F32),
            pltpu.VMEM((2, C, 256), BF16),
            pltpu.VMEM((512, OWN), BF16),
            pltpu.VMEM((3, 4, 32, X), BF16),
            pltpu.VMEM((512, 12 * X), BF16),
            pltpu.VMEM((3, C, 5 * X), BF16),
            pltpu.VMEM((3, 4, C, X), BF16),
            pltpu.VMEM((3, C, 5 * X), BF16),
            pltpu.VMEM((2, C, 2 * X), F32),
            pltpu.VMEM((2, C, X), F32),
            pltpu.VMEM((OWN, 4 * X), F32),
            pltpu.VMEM((2, 4, OWN, X), BF16),
            dma((2,)), dma((3,)), dma((3,)), dma((3,)), dma((3,)), dma, dma, dma((5,)), dma((5,)),
            dma((4, 3)), dma((4, 3)), dma((4,)), dma((4,)), dma((4, 3)), dma((4, 3)), dma((4,)), dma((4,)),
            dma, dma,
        ],
        compiler_params=pltpu.CompilerParams(
            collective_id=0, has_side_effects=True, vmem_limit_bytes=48 * 2**20
        ),
    )(
        hidden_states.reshape(128, 1280),
        modulation_shift.reshape(1, 1280),
        modulation_scale.reshape(1, 1280),
        head_weight.T,
        entry_weight.transpose(0, 1, 2, 4, 3).reshape(432, OWN),
        first_weight.reshape(2592, C),
        first_gain.reshape(1, OWN),
        second_weight.reshape(2592, C),
        second_gain.reshape(1, OWN),
    )
    return out.transpose(2, 0, 1, 3)


def solution(mesh):
    return jax.shard_map(
        body,
        mesh=mesh,
        in_specs=(
            P("segment", "band", None, "chan"),
            P("chan"),
            P("chan"),
            P("chan", None),
            P(None, None, None, "chan", None),
            P(None, None, None, "chan", None),
            P("chan"),
            P(None, None, None, "chan", None),
            P("chan"),
        ),
        out_specs=P("chan", "segment", "band", None),
        check_vma=False,
    )
```

profile of v0, /device:TPU:1, one launch (start us, length us, event | category | flops | bytes accessed | tf_op | source)
XLA Modules:
  0.0 71.1 jit_solution(11092008622688666639)
XLA Ops:
  0.0 0.7 reshape.25.shift_ref
  0.7 0.7 reshape.26.scale_ref
  1.4 0.0 copy-start
  1.4 1.6 %copy-done = bf16[3,3,3,96,384]{4,3,2,1,0:T(8,128)(2,1)S(1)} copy-done((bf16[3,3,3,96,384]{4,3,2,1,0:T(8,128)(2,1)S(1)}, bf16[3,3,3,96,384]{4,3,2,1,0:T(8,128)(2,1)}, u32[]{:S(2)}) %copy-start) | copy-done | bytes 1990680
  3.0 0.0 copy-start.1
  3.0 1.6 %copy-done.1 = bf16[3,3,3,96,384]{4,3,2,1,0:T(8,128)(2,1)S(1)} copy-done((bf16[3,3,3,96,384]{4,3,2,1,0:T(8,128)(2,1)S(1)}, bf16[3,3,3,96,384]{4,3,2,1,0:T(8,128)(2,1)}, u32[]{:S(2)}) %copy-start.1) | copy-done | bytes 1990680
  4.5 0.0 copy-start.2
  4.5 1.0 %copy-done.2 = bf16[2,1,64,1280]{3,2,1,0:T(8,128)(2,1)S(1)} copy-done((bf16[2,1,64,1280]{3,2,1,0:T(8,128)(2,1)S(1)}, bf16[2,1,64,1280]{3,2,1,0:T(8,128)(2,1)}, u32[]{:S(2)}) %copy-start.2) | copy-done | bytes 327704
  5.5 0.0 copy-start.3
  5.5 0.9 %copy-done.3 = bf16[1280,64]{0,1:T(8,128)(2,1)S(1)} copy-done((bf16[1280,64]{0,1:T(8,128)(2,1)S(1)}, bf16[1280,64]{0,1:T(8,128)(2,1)}, u32[]{:S(2)}) %copy-start.3) | copy-done | bytes 163864
  6.4 0.0 copy-start.4
  6.4 0.9 %copy-done.4 = bf16[3,3,3,96,16]{3,4,2,1,0:T(8,128)(2,1)S(1)} copy-done((bf16[3,3,3,96,16]{3,4,2,1,0:T(8,128)(2,1)S(1)}, bf16[3,3,3,96,16]{3,4,2,1,0:T(8,128)(2,1)}, u32[]{:S(2)}) %copy-start.4) | copy-done | bytes 82968
  7.3 0.0 copy-start.5
  7.3 0.7 copy-done.5
  8.0 0.0 copy-start.6
  8.0 0.7 copy-done.6
  8.6 61.8 %shard_map.91 = bf16[2,2,96,128]{3,2,1,0:T(8,128)(2,1)S(1)} custom-call(bf16[128,1280]{1,0:T(8,128)(2,1)S(1)} %bitcast.13, f32[1,1280]{1,0:T(1,128)S(1)} %reshape.25.shift_ref, f32[1,1280]{1,0:T(1,128)S(1)} %reshape.26.scale_ref, bf16[64,1280]{1,0:T(8,128)(2,1)S(1)} %bitcast.14, bf16[432,96]{1,0:T(8,128)(2,1)S(1)} %bitcast.15, ...), custom_call_target="tpu_custom_call" | custom-call | tf_op jit(solution)/shard_map/pallas_call | solution.py:281
  70.4 0.7 %copy.10 = bf16[96,2,2,128]{3,2,1,0:T(2,128)(2,1)} copy(bf16[96,2,2,128]{3,0,2,1:T(8,128)(2,1)S(1)} %bitcast.12) | data formatting | bytes 196608 | tf_op jit(solution)/shard_map/transpose | solution.py:319
Async XLA Ops:
  1.4 1.6 %copy-start = (bf16[3,3,3,96,384]{4,3,2,1,0:T(8,128)(2,1)S(1)}, bf16[3,3,3,96,384]{4,3,2,1,0:T(8,128)(2,1)}, u32[]{:S(2)}) copy-start(bf16[3,3,3,96,384]{4,3,2,1,0:T(8,128)(2,1)} %param.14) | copy-start | bytes 5971972
  3.0 1.6 %copy-start.1 = (bf16[3,3,3,96,384]{4,3,2,1,0:T(8,128)(2,1)S(1)}, bf16[3,3,3,96,384]{4,3,2,1,0:T(8,128)(2,1)}, u32[]{:S(2)}) copy-start(bf16[3,3,3,96,384]{4,3,2,1,0:T(8,128)(2,1)} %param.16) | copy-start | bytes 5971972
  4.5 1.0 %copy-start.2 = (bf16[2,1,64,1280]{3,2,1,0:T(8,128)(2,1)S(1)}, bf16[2,1,64,1280]{3,2,1,0:T(8,128)(2,1)}, u32[]{:S(2)}) copy-start(bf16[2,1,64,1280]{3,2,1,0:T(8,128)(2,1)} %param.9) | copy-start | bytes 983044
  5.5 0.9 %copy-start.3 = (bf16[1280,64]{0,1:T(8,128)(2,1)S(1)}, bf16[1280,64]{0,1:T(8,128)(2,1)}, u32[]{:S(2)}) copy-start(bf16[1280,64]{0,1:T(8,128)(2,1)} %param.12) | copy-start | bytes 491524
  6.4 0.9 %copy-start.4 = (bf16[3,3,3,96,16]{3,4,2,1,0:T(8,128)(2,1)S(1)}, bf16[3,3,3,96,16]{3,4,2,1,0:T(8,128)(2,1)}, u32[]{:S(2)}) copy-start(bf16[3,3,3,96,16]{3,4,2,1,0:T(8,128)(2,1)} %param.13) | copy-start | bytes 248836
  7.3 0.7 copy-start.5
  8.0 0.7 copy-start.6
where the time goes:
time: 71.5 us; the launch traced here: 71.1 us
  Pallas kernels  61.8 us (86%)
  local copies, waits for them, and re-layouts  9.32 us (13%)
    pallas_call x1, Pallas kernels, body(): pl.pallas_call(kernel, out_shape=jax.ShapeDtypeStruct((2, 2, OWN, X), BF1...  61.8 us
    unnamed x14, local copies, waits for them, and re-layouts  7.2 us

commit v1 on v0

v1 whole, which is shorter than its diff:
```python
import jax
import jax.numpy as jnp
from jax import lax
from jax.experimental import pallas as pl
from jax.experimental.pallas import tpu as pltpu
from jax.sharding import PartitionSpec as P

D = 5120
C = 384
EPS = 1e-6
OWN = 96
X = 128
MESH = pl.DeviceIdType.MESH
NT = (((1,), (1,)), ((), ()))
F32 = jnp.float32
BF16 = jnp.bfloat16


def iota(shape, axis):
    return lax.broadcasted_iota(jnp.int32, shape, axis)


def column(row, rows):
    eye = iota((rows, X), 0) == iota((rows, X), 1)
    return jnp.sum(jnp.where(eye, jnp.broadcast_to(row, (rows, X)), 0.0), axis=1, keepdims=True)


def as_row(col):
    rows = col.shape[0]
    eye = iota((rows, X), 0) == iota((rows, X), 1)
    return jnp.sum(jnp.where(eye, jnp.broadcast_to(col, (rows, X)), 0.0), axis=0, keepdims=True)


def lanes_of(ref):
    return jnp.concatenate([ref[j : j + 1, :] for j in range(10)], axis=1)


def silu_norm(values, gain):
    power = jnp.sum(values * values, axis=0, keepdims=True) / C
    scaled = values * lax.rsqrt(power + EPS) * gain
    return (scaled * (0.5 * jnp.tanh(0.5 * scaled) + 0.5)).astype(BF16)


def kernel(
    h_hbm, shift_hbm, scale_hbm, wt_hbm, ew_hbm, w1_hbm, g1_hbm, w2_hbm, g2_hbm,
    out_ref,
    h_ref, shift_ref, scale_ref, wt_ref, g1_ref, g2_ref, w1, w2, parts, ewg, ewp, lat, cols, act1, raw, act2, total, gains, resid, fin,
    wsem, s_p, r_p, s_e, r_e, s_es, r_es, s_l, r_l, s_g, r_g, s_o, r_o, s_h, r_h, s_s, r_s, s_f, r_f,
):
    s, b, c = lax.axis_index("segment"), lax.axis_index("band"), lax.axis_index("chan")
    bands = lax.axis_size("band")
    up, down = lax.rem(b + 1, bands), lax.rem(b + bands - 1, bands)
    zpeers = [(s, b, lax.rem(c + d, 4)) for d in (1, 2, 3)]
    sibling = (1 - s, b, c)
    outer = (1 - s, jnp.where(s == 0, down, up), c)
    y = lax.rem(b, 4)
    apart = jnp.where(s == 0, y == 0, y == 3)
    passes = (y == 1) | (y == 2)
    goal = (2 - y, lax.rem(b + jnp.where(y == 2, 2, bands - 2), bands), c)
    skipped = lax.rem(b + jnp.where(s == 0, bands - 2, 2), bands)
    far = [(s, up, c), (1 - s, up, c), (s, down, c), (1 - s, down, c)]

    pairs = (
        (wt_hbm, wt_ref), (scale_hbm, scale_ref), (shift_hbm, shift_ref), (h_hbm, h_ref), (g1_hbm, g1_ref), (g2_hbm, g2_ref),
        (ew_hbm, ewp.at[pl.ds(0, 432)]), (w1_hbm, w1), (w2_hbm, w2),
    )
    loads = [pltpu.make_async_copy(src, dst, wsem.at[i]) for i, (src, dst) in enumerate(pairs)]
    for load in loads:
        load.start()
    barrier = pltpu.get_barrier_semaphore()
    for peer in zpeers + [sibling] + far:
        pl.semaphore_signal(barrier, inc=1, device_id=peer, device_id_type=MESH)

    @pl.when(apart)
    def _():
        for seg in range(2):
            pl.semaphore_signal(barrier, inc=1, device_id=(seg, skipped, c), device_id_type=MESH)


    def ready(src, dst, send, recv, peer):
        return pltpu.make_async_remote_copy(
            src_ref=src, dst_ref=dst, send_sem=send, recv_sem=recv, device_id=peer, device_id_type=MESH
        )

    def remote(*ends):
        copy = ready(*ends)
        copy.start()
        return copy

    sent = []

    order = iota((64, 64), 0)
    source = 4 * lax.rem(order, 16) + 2 * lax.rem(order // 16, 2) + order // 32
    permute = (iota((64, 64), 1) == source).astype(F32).astype(BF16)
    for load in loads[:3]:
        load.wait()
    weight = jnp.dot(permute, wt_ref[...], preferred_element_type=F32)
    raised = weight * (1.0 + lanes_of(scale_ref))
    high = raised.astype(BF16)
    low = (raised - high.astype(F32)).astype(BF16)
    for load in loads[3:6]:
        load.wait()
    both = lax.dot_general(jnp.concatenate([high, low], axis=0), h_ref[...], NT, preferred_element_type=F32)
    states = h_ref[...].astype(F32)
    parts[c] = jnp.zeros((72, X), F32)
    parts[c, 0:64, :] = both[0:64] + both[64:128]
    parts[c, 64:65, :] = as_row(jnp.sum(states, axis=1, keepdims=True))
    parts[c, 65:66, :] = as_row(jnp.sum(states * states, axis=1, keepdims=True))
    parts[c, 66:67, :] = as_row(jnp.sum(high.astype(F32) + low.astype(F32), axis=1, keepdims=True))
    parts[c, 67:68, :] = as_row(jnp.sum(weight * lanes_of(shift_ref), axis=1, keepdims=True))
    parts[c, 68:69, 0:OWN] = g1_ref[...]
    parts[c, 69:70, 0:OWN] = g2_ref[...]

    pl.semaphore_wait(barrier, 8 + passes.astype(jnp.int32))
    first = [remote(parts.at[c], parts.at[c], s_p.at[d], r_p.at[d], zpeers[d]) for d in range(3)]
    sent += first

    own_rows = pl.ds(pl.multiple_of(c * OWN, OWN), OWN)
    loads[6].wait()
    ewp[432:512, :] = jnp.zeros((80, OWN), BF16)
    eye96 = (iota((OWN, OWN), 0) == iota((OWN, OWN), 1)).astype(F32).astype(BF16)
    half = ewp[pl.ds(pl.multiple_of(s * 256, 256), 256), :]
    ewg[s, own_rows, :] = lax.dot_general(eye96, half, NT, preferred_element_type=F32).astype(BF16)
    gather_e = [
        remote(ewg.at[s, own_rows], ewg.at[s, own_rows], s_e.at[d], r_e.at[d], zpeers[d]) for d in range(3)
    ]
    sent += gather_e

    zero = jnp.zeros((16, X), BF16)
    for e in range(4):
        for f in range(4):
            at = (e * 4 + f) * X
            cols[432:512, at : at + X] = jnp.zeros((80, X), BF16)
            for p in range(2 - f):
                for qr in range(9):
                    k = (p * 9 + qr) * 16
                    cols[k : k + 16, at : at + X] = zero
        act1[e, :, 0:X] = jnp.zeros((C, X), BF16)
    for slot in range(3):
        act2[slot, :, 0:X] = jnp.zeros((C, X), BF16)

    @pl.when(~apart)
    def _():
        lat[4 * s] = jnp.zeros((4, 32, X), BF16)

    for copy in first:
        copy.wait_recv()
    summed = (parts[0] + parts[1]) + (parts[2] + parts[3])
    center = summed[64:65] / D
    spread = summed[65:66] / D - center * center
    head = (summed[0:64] - column(summed[66:67], 64) * center) * lax.rsqrt(spread + EPS) + column(
        summed[67:68], 64
    )
    head = head.astype(BF16)
    even = lax.rem(iota((32, X), 1), 2) == 0
    for t in range(2):
        spreadout = (iota((X, X), 0) == t * 64 + iota((X, X), 1) // 2).astype(F32).astype(BF16)
        wide = jnp.dot(head, spreadout, preferred_element_type=F32)
        lat[2, 2 * s + t] = jnp.where(even, wide[0:32], wide[32:64]).astype(BF16)
    mine = pl.ds(2 * s, 2)
    whole, row0, row1 = pl.ds(0, 32), pl.ds(0, 16), pl.ds(16, 16)

    def latent(slot, rows, j, arrives, peer):
        return ready(lat.at[2, mine, rows], lat.at[slot, mine, rows], s_l.at[j], r_l.at[arrives], peer)

    latents = [
        latent(1, whole, 1, 1 + s, (0, up, c)),
        latent(1, row1, 2, 1 + s, (1, up, c)),
        latent(3, row0, 3, 3 + s, (0, down, c)),
        latent(3, whole, 4, 3 + s, (1, down, c)),
        latent(2, whole, 0, 0, sibling),
    ]
    beyond = (latent(0, row1, 5, 5 + s, goal), latent(4, row0, 5, 5 + s, goal))
    for seg in range(2):
        pl.when(passes & (goal[0] == seg))(beyond[seg].start)
    for copy in latents:
        copy.start()
    sent += latents
    for chan in range(4):
        for g in range(2):
            row = parts[chan, 68 + g : 69 + g, :]
            gains[g, chan * OWN : (chan + 1) * OWN, :] = jnp.broadcast_to(column(row, OWN), (OWN, X))

    for copy in gather_e:
        copy.wait_recv()
    share = remote(ewg.at[s], ewg.at[s], s_es, r_es, sibling)
    sent.append(share)
    latents[4].wait_recv()
    for seg in range(2):

        @pl.when(s == seg)
        def _():
            for slot, rows in ((1, (whole, row1)[seg]), (3, (row0, whole)[seg])):
                for source_seg in range(2):
                    latent(slot, rows, 1, slot + source_seg, sibling).wait_recv()

        @pl.when(apart & (s == seg))
        def _():
            for source_seg in range(2):
                latent(4 * seg, (row1, row0)[seg], 5, 5 + source_seg, sibling).wait_recv()


    @pl.when(b == 0)
    def _():
        lat[1] = jnp.zeros((4, 32, X), BF16)

    @pl.when(b == bands - 1)
    def _():
        lat[3] = jnp.zeros((4, 32, X), BF16)

    lane = iota((16, X), 1)
    for k in range(6):
        slot, a = s + (1 + k) // 2, (1 + k) % 2
        for f in range(4):
            tile = lat[slot, f, a * 16 : a * 16 + 16, :]
            wide = tile.astype(F32)
            shifted = [
                jnp.where(lane == 0, 0.0, pltpu.roll(wide, 1, 1)).astype(BF16),
                tile,
                jnp.where(lane == X - 1, 0.0, pltpu.roll(wide, X - 1, 1)).astype(BF16),
            ]
            for p in range(3):
                for q in range(3):
                    e, g = k - q, f + 2 - p
                    if 0 <= e < 4 and g < 4:
                        for r in range(3):
                            row = ((p * 3 + q) * 3 + r) * 16
                            at = (e * 4 + g) * X
                            cols[row : row + 16, at : at + X] = shifted[r]

    share.wait_recv()
    row_at = 2 * b + 2 * s - 2
    for e in range(4):
        for pair in range(2):
            at = (e * 4 + pair * 2) * X
            value = jnp.dot(ewg[0], cols[0:256, at : at + 2 * X], preferred_element_type=F32)
            value += jnp.dot(ewg[1], cols[256:512, at : at + 2 * X], preferred_element_type=F32)
            rounded = value.astype(BF16)
            if e in (1, 2):

                @pl.when(s == 2 - e)
                def _():
                    total[0, :, 0 : 2 * X] = rounded.astype(F32)
                    resid[:, pair * 2 * X : (pair + 1) * 2 * X] = total[0, own_rows, 0 : 2 * X]

            valid = (row_at + e >= 0) & (row_at + e < 2 * bands)
            for t in range(2):
                done = silu_norm(rounded[:, t * X : (t + 1) * X].astype(F32), gains[0])
                lanes = (pair * 2 + t + 1) * X
                act1[e, :, lanes : lanes + X] = jnp.where(valid, done, jnp.zeros_like(done))

    def taps(weights, acts, q, pair, slot=None):
        slot = q if slot is None else slot
        value = None
        for p in range(1 if pair == 0 else 0, 3):
            lanes = (pair * 2 + p - 1) * X
            rows = pl.ds(pl.multiple_of((p * 3 + q) * 288, 288), 288)
            term = jnp.dot(weights[rows, :], acts[slot, :, lanes : lanes + 2 * X], preferred_element_type=F32)
            value = term if value is None else value + term
        return value

    lane96 = iota((OWN, X), 1)

    def join(value, t):
        lanes = slice(t * X, (t + 1) * X)
        left = jnp.where(lane96 == 0, 0.0, pltpu.roll(value[0:OWN, lanes], 1, 1))
        right = jnp.where(lane96 == X - 1, 0.0, pltpu.roll(value[2 * OWN : 3 * OWN, lanes], X - 1, 1))
        return left + value[OWN : 2 * OWN, lanes] + right

    near, away = 2 - 2 * s, 2 * s
    loads[7].wait()
    own_gather, across, halo, to_sibling = [], [], [], []
    for f in range(4):
        tile, passed = raw.at[1, f, own_rows], raw.at[away, f, own_rows]
        own_gather.append([ready(tile, tile, s_g.at[f, d], r_g.at[f, d], zpeers[d]) for d in range(3)])
        halo.append([ready(passed, passed, s_h.at[f, d], r_h.at[f, d], zpeers[d]) for d in range(3)])
        to_sibling.append(ready(raw.at[1, f], raw.at[away, f], s_s.at[f], r_s.at[f], sibling))
        across.append(ready(raw.at[1, f], raw.at[near, f], s_o.at[f], r_o.at[f], outer))

    def middle_row(start, slot, copies):
        for pair in range(2):
            value = None
            for q in range(3):
                term = taps(w1, act1, q, pair, start + q)
                value = term if value is None else value + term
            for t in range(2):
                f = pair * 2 + t
                raw[slot, f, own_rows, :] = join(value, t).astype(BF16)
                for copy in copies[f]:
                    copy.start()

    middle_row(1 - s, 1, own_gather)

    @pl.when(apart)
    def _():
        middle_row(s, away, halo)

    def activate(slot, f, valid):
        done = silu_norm(raw[slot, f].astype(F32), gains[1])
        lanes = (f + 1) * X
        act2[slot, :, lanes : lanes + X] = jnp.where(valid, done, jnp.zeros_like(done))

    for f in range(4):
        for copy in own_gather[f]:
            copy.wait_recv()
        to_sibling[f].start()
        pl.when(~apart)(across[f].start)
        activate(1, f, True)
    loads[8].wait()
    for pair in range(2):
        total[pair, 0:288, 0 : 2 * X] = taps(w2, act2, 1, pair)
    for f in range(4):
        to_sibling[f].wait_recv()
        activate(near, f, True)
    for pair in range(2):
        total[pair, 0:288, 0 : 2 * X] += taps(w2, act2, near, pair)
    inside = jnp.where(s == 0, b > 0, b < bands - 1)
    finals = []
    for pair in range(2):
        for f in (2 * pair, 2 * pair + 1):

            @pl.when(apart)
            def _():
                for copy in halo[f]:
                    copy.wait_recv()

            pl.when(~apart)(across[f].wait_recv)
            activate(away, f, inside)
        value = total[pair, 0:288, 0 : 2 * X] + taps(w2, act2, away, pair)
        for t in range(2):
            f = pair * 2 + t
            decoded = (resid[:, f * X : (f + 1) * X] + join(value, t)).astype(BF16)
            fin[0, f] = decoded
    sections = remote(
        fin.at[0, pl.ds(2 * (1 - s), 2)], fin.at[1, pl.ds(2 * (1 - s), 2)], s_f, r_f, sibling
    )
    sent.append(sections)
    for t in range(2):
        out_ref[t, s] = fin[0, 2 * s + t]
    sections.wait_recv()
    for t in range(2):
        out_ref[t, 1 - s] = fin[1, 2 * s + t]
    for seg in range(2):
        pl.when(passes & (goal[0] == seg))(beyond[seg].wait_send)
    for copy in sent + sum(own_gather, []) + to_sibling:
        copy.wait_send()

    @pl.when(apart)
    def _():
        for copy in sum(halo, []):
            copy.wait_send()

    @pl.when(~apart)
    def _():
        for copy in across:
            copy.wait_send()


def body(
    hidden_states, modulation_shift, modulation_scale, head_weight, entry_weight,
    first_weight, first_gain, second_weight, second_gain,
):
    vmem = pl.BlockSpec(memory_space=pltpu.VMEM)
    hbm = pl.BlockSpec(memory_space=pltpu.HBM)
    dma = pltpu.SemaphoreType.DMA
    out = pl.pallas_call(
        kernel,
        out_shape=jax.ShapeDtypeStruct((2, 2, OWN, X), BF16),
        in_specs=[hbm] * 9,
        out_specs=vmem,
        scratch_shapes=[
            pltpu.VMEM((128, 1280), BF16),
            pltpu.VMEM((10, X), F32),
            pltpu.VMEM((10, X), F32),
            pltpu.VMEM((64, 1280), BF16),
            pltpu.VMEM((1, OWN), F32),
            pltpu.VMEM((1, OWN), F32),
            pltpu.VMEM((2592, C), BF16),
            pltpu.VMEM((2592, C), BF16),
            pltpu.VMEM((4, 72, X), F32),
            pltpu.VMEM((2, C, 256), BF16),
            pltpu.VMEM((512, OWN), BF16),
            pltpu.VMEM((5, 4, 32, X), BF16),
            pltpu.VMEM((512, 16 * X), BF16),
            pltpu.VMEM((4, C, 5 * X), BF16),
            pltpu.VMEM((3, 4, C, X), BF16),
            pltpu.VMEM((3, C, 5 * X), BF16),
            pltpu.VMEM((2, C, 2 * X), F32),
            pltpu.VMEM((2, C, X), F32),
            pltpu.VMEM((OWN, 4 * X), F32),
            pltpu.VMEM((2, 4, OWN, X), BF16),
            dma((9,)), dma((3,)), dma((3,)), dma((3,)), dma((3,)), dma, dma, dma((6,)), dma((7,)),
            dma((4, 3)), dma((4, 3)), dma((4,)), dma((4,)), dma((4, 3)), dma((4, 3)), dma((4,)), dma((4,)),
            dma, dma,
        ],
        compiler_params=pltpu.CompilerParams(
            collective_id=0, has_side_effects=True, vmem_limit_bytes=63 * 2**20
        ),
    )(
        hidden_states.reshape(128, 1280),
        modulation_shift.reshape(10, X),
        modulation_scale.reshape(10, X),
        head_weight.T,
        entry_weight.transpose(0, 1, 2, 4, 3).reshape(432, OWN),
        first_weight.reshape(2592, C),
        first_gain.reshape(1, OWN),
        second_weight.reshape(2592, C),
        second_gain.reshape(1, OWN),
    )
    return out.transpose(2, 0, 1, 3)


def solution(mesh):
    return jax.shard_map(
        body,
        mesh=mesh,
        in_specs=(
            P("segment", "band", None, "chan"),
            P("chan"),
            P("chan"),
            P("chan", None),
            P(None, None, None, "chan", None),
            P(None, None, None, "chan", None),
            P("chan"),
            P(None, None, None, "chan", None),
            P("chan"),
        ),
        out_specs=P("chan", "segment", "band", None),
        check_vma=False,
    )
```

time: 71.5 us -> 51.2 us (0.72)
  Pallas kernels: 61.8 us -> 49.5 us
  local copies, waits for them, and re-layouts: 9.32 us -> 1.61 us
    pallas_call x1, Pallas kernels: 61.8 us -> 49.5 us  [body(): pl.pallas_call(kernel, out_shape=jax.ShapeDtypeStruct((2, 2, OWN, X), BF1...]
    unnamed x14 -> x0, local copies, waits for them, and re-layouts: 7.2 us -> none
    reshape x2 -> x0, local copies, waits for them, and re-layouts: 1.4 us -> none  [the longest x1 0.7 us: body(): modulation_shift.reshape(1, 1280)]
    transpose x1, local copies, waits for them, and re-layouts: 0.72 us -> 1.61 us  [body(): return out.transpose(2, 0, 1, 3)]
where the time goes in v1:
time: 51.2 us; the launch traced here: 51.1 us
  Pallas kernels  49.5 us (97%)
  local copies, waits for them, and re-layouts  1.61 us (3%)
    pallas_call x1, Pallas kernels, body(): pl.pallas_call(kernel, out_shape=jax.ShapeDtypeStruct((2, 2, OWN, X), BF1...  49.5 us
    transpose x1, local copies, waits for them, and re-layouts, body(): return out.transpose(2, 0, 1, 3)  1.61 us

profile of v1, /device:TPU:1, one launch (start us, length us, event | category | flops | bytes accessed | tf_op | source)
XLA Modules:
  0.0 51.1 jit_solution(4382629207646965987)
XLA Ops:
  0.0 49.5 %shard_map.91 = bf16[2,2,96,128]{3,2,1,0:T(8,128)(2,1)} custom-call(bf16[128,1280]{1,0:T(8,128)(2,1)} %bitcast.15, f32[10,128]{1,0:T(8,128)} %bitcast.18, f32[10,128]{1,0:T(8,128)} %bitcast.19, bf16[64,1280]{1,0:T(8,128)(2,1)} %bitcast.16, bf16[432,96]{1,0:T(8,128)(2,1)} %bitcast.17, bf16[2592,384]{1,0:T(8,128)(2,1)} %bitcast.12, f32[1,96]{1,0:T(1,128)} %bitcast.20, ...), custom_call_target="tpu_custom_call" | custom-call | tf_op jit(solution)/shard_map/pallas_call | solution.py:366
  49.5 1.6 %copy.10 = bf16[96,2,2,128]{3,2,1,0:T(2,128)(2,1)} copy(bf16[96,2,2,128]{3,0,2,1:T(8,128)(2,1)} %bitcast.14) | data formatting | bytes 196608 | tf_op jit(solution)/shard_map/transpose | solution.py:410

commit v2 on v1

--- a/solution.py
+++ b/solution.py
@@ -44,7 +44,7 @@
 def kernel(
     h_hbm, shift_hbm, scale_hbm, wt_hbm, ew_hbm, w1_hbm, g1_hbm, w2_hbm, g2_hbm,
     out_ref,
-    h_ref, shift_ref, scale_ref, wt_ref, g1_ref, g2_ref, w1, w2, parts, ewg, ewp, lat, cols, act1, raw, act2, total, gains, resid, fin,
+    h_ref, shift_ref, scale_ref, wt_ref, g1_ref, g2_ref, w1, w2, parts, exact, stats, ewg, ewp, lat, cols, act1, raw, act2, total, gains, resid, fin,
     wsem, s_p, r_p, s_e, r_e, s_es, r_es, s_l, r_l, s_g, r_g, s_o, r_o, s_h, r_h, s_s, r_s, s_f, r_f,
 ):
     s, b, c = lax.axis_index("segment"), lax.axis_index("band"), lax.axis_index("chan")
@@ -60,6 +60,16 @@
     skipped = lax.rem(b + jnp.where(s == 0, bands - 2, 2), bands)
     far = [(s, up, c), (1 - s, up, c), (s, down, c), (1 - s, down, c)]
 
+    barrier = pltpu.get_barrier_semaphore()
+    for peer in far + zpeers + [sibling]:
+        pl.semaphore_signal(barrier, inc=1, device_id=peer, device_id_type=MESH)
+
+    @pl.when(apart)
+    def _():
+        for seg in range(2):
+            pl.semaphore_signal(barrier, inc=1, device_id=(seg, skipped, c), device_id_type=MESH)
+
+
     pairs = (
         (wt_hbm, wt_ref), (scale_hbm, scale_ref), (shift_hbm, shift_ref), (h_hbm, h_ref), (g1_hbm, g1_ref), (g2_hbm, g2_ref),
         (ew_hbm, ewp.at[pl.ds(0, 432)]), (w1_hbm, w1), (w2_hbm, w2),
@@ -67,15 +77,6 @@
     loads = [pltpu.make_async_copy(src, dst, wsem.at[i]) for i, (src, dst) in enumerate(pairs)]
     for load in loads:
         load.start()
-    barrier = pltpu.get_barrier_semaphore()
-    for peer in zpeers + [sibling] + far:
-        pl.semaphore_signal(barrier, inc=1, device_id=peer, device_id_type=MESH)
-
-    @pl.when(apart)
-    def _():
-        for seg in range(2):
-            pl.semaphore_signal(barrier, inc=1, device_id=(seg, skipped, c), device_id_type=MESH)
-
 
     def ready(src, dst, send, recv, peer):
         return pltpu.make_async_remote_copy(
@@ -102,17 +103,21 @@
         load.wait()
     both = lax.dot_general(jnp.concatenate([high, low], axis=0), h_ref[...], NT, preferred_element_type=F32)
     states = h_ref[...].astype(F32)
-    parts[c] = jnp.zeros((72, X), F32)
-    parts[c, 0:64, :] = both[0:64] + both[64:128]
-    parts[c, 64:65, :] = as_row(jnp.sum(states, axis=1, keepdims=True))
-    parts[c, 65:66, :] = as_row(jnp.sum(states * states, axis=1, keepdims=True))
-    parts[c, 66:67, :] = as_row(jnp.sum(high.astype(F32) + low.astype(F32), axis=1, keepdims=True))
-    parts[c, 67:68, :] = as_row(jnp.sum(weight * lanes_of(shift_ref), axis=1, keepdims=True))
-    parts[c, 68:69, 0:OWN] = g1_ref[...]
-    parts[c, 69:70, 0:OWN] = g2_ref[...]
+    sums = as_row(jnp.sum(states, axis=1, keepdims=True))
+    lift = jnp.sum(high.astype(F32) + low.astype(F32), axis=1, keepdims=True)
+    exact[...] = both[0:64] + both[64:128] - lift * (sums / 1280)
+    parts[c] = exact[...].astype(BF16)
+    stats[c] = jnp.zeros((8, X), F32)
+    stats[c, 0:1, :] = sums
+    stats[c, 1:2, :] = as_row(jnp.sum(states * states, axis=1, keepdims=True))
+    stats[c, 2:3, :] = as_row(lift)
+    stats[c, 3:4, :] = as_row(jnp.sum(weight * lanes_of(shift_ref), axis=1, keepdims=True))
+    stats[c, 4:5, 0:OWN] = g1_ref[...]
+    stats[c, 5:6, 0:OWN] = g2_ref[...]
 
     pl.semaphore_wait(barrier, 8 + passes.astype(jnp.int32))
-    first = [remote(parts.at[c], parts.at[c], s_p.at[d], r_p.at[d], zpeers[d]) for d in range(3)]
+    first = [remote(parts.at[c], parts.at[c], s_p.at[d], r_p.at[d], zpeers[d]) for d in (1, 0, 2)]
+    first += [remote(stats.at[c], stats.at[c], s_p.at[3 + d], r_p.at[3 + d], zpeers[d]) for d in (1, 0, 2)]
     sent += first
 
     own_rows = pl.ds(pl.multiple_of(c * OWN, OWN), OWN)
@@ -145,12 +150,15 @@
 
     for copy in first:
         copy.wait_recv()
-    summed = (parts[0] + parts[1]) + (parts[2] + parts[3])
-    center = summed[64:65] / D
-    spread = summed[65:66] / D - center * center
-    head = (summed[0:64] - column(summed[66:67], 64) * center) * lax.rsqrt(spread + EPS) + column(
-        summed[67:68], 64
-    )
+    summed = (stats[0] + stats[1]) + (stats[2] + stats[3])
+    center = summed[0:1] / D
+    spread = summed[1:2] / D - center * center
+    terms = [
+        jnp.where(c == chan, exact[...], parts[chan].astype(F32)) + column(stats[chan, 2:3, :], 64) * (stats[chan, 0:1, :] / 1280 - center)
+        for chan in range(4)
+    ]
+    head = (terms[0] + terms[1]) + (terms[2] + terms[3])
+    head = head * lax.rsqrt(spread + EPS) + column(summed[3:4], 64)
     head = head.astype(BF16)
     even = lax.rem(iota((32, X), 1), 2) == 0
     for t in range(2):
@@ -178,7 +186,7 @@
     sent += latents
     for chan in range(4):
         for g in range(2):
-            row = parts[chan, 68 + g : 69 + g, :]
+            row = stats[chan, 4 + g : 5 + g, :]
             gains[g, chan * OWN : (chan + 1) * OWN, :] = jnp.broadcast_to(column(row, OWN), (OWN, X))
 
     for copy in gather_e:
@@ -209,53 +217,50 @@
         lat[3] = jnp.zeros((4, 32, X), BF16)
 
     lane = iota((16, X), 1)
-    for k in range(6):
-        slot, a = s + (1 + k) // 2, (1 + k) % 2
-        for f in range(4):
-            tile = lat[slot, f, a * 16 : a * 16 + 16, :]
-            wide = tile.astype(F32)
-            shifted = [
-                jnp.where(lane == 0, 0.0, pltpu.roll(wide, 1, 1)).astype(BF16),
-                tile,
-                jnp.where(lane == X - 1, 0.0, pltpu.roll(wide, X - 1, 1)).astype(BF16),
-            ]
-            for p in range(3):
-                for q in range(3):
-                    e, g = k - q, f + 2 - p
-                    if 0 <= e < 4 and g < 4:
-                        for r in range(3):
-                            row = ((p * 3 + q) * 3 + r) * 16
-                            at = (e * 4 + g) * X
-                            cols[row : row + 16, at : at + X] = shifted[r]
-
-    share.wait_recv()
+
+    def windows(lo, n):
+        for k in range(6):
+            slot, a = s + (1 + k) // 2, (1 + k) % 2
+            for f in range(lo + n):
+                tile = lat[slot, f, a * 16 : a * 16 + 16, :]
+                wide = tile.astype(F32)
+                shifted = [
+                    jnp.where(lane == 0, 0.0, pltpu.roll(wide, 1, 1)).astype(BF16),
+                    tile,
+                    jnp.where(lane == X - 1, 0.0, pltpu.roll(wide, X - 1, 1)).astype(BF16),
+                ]
+                for p in range(3):
+                    for q in range(3):
+                        e, g = k - q, f + 2 - p
+                        if 0 <= e < 4 and lo <= g < lo + n:
+                            for r in range(3):
+                                row = ((p * 3 + q) * 3 + r) * 16
+                                at = (e * 4 + g) * X
+                                cols[row : row + 16, at : at + X] = shifted[r]
+
     row_at = 2 * b + 2 * s - 2
-    for e in range(4):
-        for pair in range(2):
-            at = (e * 4 + pair * 2) * X
-            value = jnp.dot(ewg[0], cols[0:256, at : at + 2 * X], preferred_element_type=F32)
-            value += jnp.dot(ewg[1], cols[256:512, at : at + 2 * X], preferred_element_type=F32)
-            rounded = value.astype(BF16)
-            if e in (1, 2):
-
-                @pl.when(s == 2 - e)
-                def _():
-                    total[0, :, 0 : 2 * X] = rounded.astype(F32)
-                    resid[:, pair * 2 * X : (pair + 1) * 2 * X] = total[0, own_rows, 0 : 2 * X]
-
-            valid = (row_at + e >= 0) & (row_at + e < 2 * bands)
-            for t in range(2):
-                done = silu_norm(rounded[:, t * X : (t + 1) * X].astype(F32), gains[0])
-                lanes = (pair * 2 + t + 1) * X
-                act1[e, :, lanes : lanes + X] = jnp.where(valid, done, jnp.zeros_like(done))
-
-    def taps(weights, acts, q, pair, slot=None):
+
+    def entry_row(e, lo, n, own=False):
+        at = pl.ds(pl.multiple_of((e * 4 + lo) * X, n * X), n * X)
+        value = jnp.dot(ewg[0], cols[0:256, at], preferred_element_type=F32)
+        value += jnp.dot(ewg[1], cols[256:512, at], preferred_element_type=F32)
+        rounded = value.astype(BF16)
+        if own:
+            total[0, :, 0 : n * X] = rounded.astype(F32)
+            resid[:, lo * X : (lo + n) * X] = total[0, own_rows, 0 : n * X]
+        valid = (row_at + e >= 0) & (row_at + e < 2 * bands)
+        for t in range(n):
+            done = silu_norm(rounded[:, t * X : (t + 1) * X].astype(F32), gains[0])
+            lanes = (lo + t + 1) * X
+            act1[e, :, lanes : lanes + X] = jnp.where(valid, done, jnp.zeros_like(done))
+
+    def taps(weights, acts, q, lo, n, slot=None):
         slot = q if slot is None else slot
         value = None
-        for p in range(1 if pair == 0 else 0, 3):
-            lanes = (pair * 2 + p - 1) * X
+        for p in range(max(0, 3 - lo - n), 3):
+            lanes = (lo + p - 1) * X
             rows = pl.ds(pl.multiple_of((p * 3 + q) * 288, 288), 288)
-            term = jnp.dot(weights[rows, :], acts[slot, :, lanes : lanes + 2 * X], preferred_element_type=F32)
+            term = jnp.dot(weights[rows, :], acts[slot, :, lanes : lanes + n * X], preferred_element_type=F32)
             value = term if value is None else value + term
         return value
 
@@ -268,87 +273,148 @@
         return left + value[OWN : 2 * OWN, lanes] + right
 
     near, away = 2 - 2 * s, 2 * s
-    loads[7].wait()
-    own_gather, across, halo, to_sibling = [], [], [], []
-    for f in range(4):
-        tile, passed = raw.at[1, f, own_rows], raw.at[away, f, own_rows]
-        own_gather.append([ready(tile, tile, s_g.at[f, d], r_g.at[f, d], zpeers[d]) for d in range(3)])
-        halo.append([ready(passed, passed, s_h.at[f, d], r_h.at[f, d], zpeers[d]) for d in range(3)])
-        to_sibling.append(ready(raw.at[1, f], raw.at[away, f], s_s.at[f], r_s.at[f], sibling))
-        across.append(ready(raw.at[1, f], raw.at[near, f], s_o.at[f], r_o.at[f], outer))
-
-    def middle_row(start, slot, copies):
-        for pair in range(2):
-            value = None
-            for q in range(3):
-                term = taps(w1, act1, q, pair, start + q)
-                value = term if value is None else value + term
-            for t in range(2):
-                f = pair * 2 + t
-                raw[slot, f, own_rows, :] = join(value, t).astype(BF16)
-                for copy in copies[f]:
+    between = (c == 1) | (c == 2)
+    relayed = 4
+
+    class Gather:
+        def __init__(self, f, slot, sends, recvs):
+            tile = raw.at[slot, f, own_rows]
+            self.out = [ready(tile, tile, sends.at[f, d], recvs.at[f, c], zpeers[d]) for d in range(3)]
+            self.into = [
+                ready(tile, tile, sends.at[f, d], recvs.at[f, lax.rem(c + d + 1, 4)], zpeers[d]) for d in range(3)
+            ]
+            self.direct = [c != 3, None, c != 0] if f < relayed else [None, None, None]
+            source = 3 * (2 - c)
+            end = raw.at[slot, f, pl.ds(pl.multiple_of(jnp.where(between, source, c) * OWN, OWN), OWN)]
+            self.relay = None
+            if f < relayed:
+                goal_chan = jnp.where(between, 3 * (c - 1), lax.rem(c + 1, 4))
+                self.relay = ready(
+                    end, end, sends.at[f, 3], recvs.at[f, jnp.where(between, source, c)], (s, b, goal_chan)
+                )
+
+        def start(self):
+            for copy, when in zip(self.out, self.direct):
+                if when is None:
                     copy.start()
-
-    middle_row(1 - s, 1, own_gather)
-
-    @pl.when(apart)
-    def _():
-        middle_row(s, away, halo)
+                else:
+                    pl.when(when)(copy.start)
+
+        def arrive(self):
+            self.into[1].wait_recv()
+            if self.relay is not None:
+                pl.when(between)(self.relay.start)
+            self.into[0].wait_recv()
+            self.into[2].wait_recv()
+
+        def sent(self):
+            for copy, when in zip(self.out, self.direct):
+                if when is None:
+                    copy.wait_send()
+                else:
+                    pl.when(when)(copy.wait_send)
+            if self.relay is not None:
+                pl.when(between)(self.relay.wait_send)
+
+    own_gather = [Gather(f, 1, s_g, r_g) for f in range(4)]
+    halo = [Gather(f, away, s_h, r_h) for f in range(4)]
+    to_sibling = [ready(raw.at[1, f], raw.at[away, f], s_s.at[f], r_s.at[f], sibling) for f in range(4)]
+    across = [ready(raw.at[1, f], raw.at[near, f], s_o.at[f], r_o.at[f], outer) for f in range(4)]
+
+    def middle_row(start, slot, lo, n, copies):
+        value = None
+        for q in range(3):
+            term = taps(w1, act1, q, lo, n, start + q)
+            value = term if value is None else value + term
+        for t in range(n):
+            f = lo + t
+            raw[slot, f, own_rows, :] = join(value, t).astype(BF16)
+            copies[f].start()
+
+    for lo, n in ((0, 2), (2, 2)):
+        windows(lo, n)
+        if lo == 0:
+            share.wait_recv()
+        for k in range(3):
+            entry_row(1 - s + k, lo, n, own=k == 1)
+        if lo == 0:
+            loads[7].wait()
+        middle_row(1 - s, 1, lo, n, own_gather)
+
+        @pl.when(apart)
+        def _():
+            entry_row(3 * s, lo, n)
+            middle_row(s, away, lo, n, halo)
 
     def activate(slot, f, valid):
         done = silu_norm(raw[slot, f].astype(F32), gains[1])
         lanes = (f + 1) * X
         act2[slot, :, lanes : lanes + X] = jnp.where(valid, done, jnp.zeros_like(done))
 
-    for f in range(4):
-        for copy in own_gather[f]:
-            copy.wait_recv()
+    inside = jnp.where(s == 0, b > 0, b < bands - 1)
+
+    def own_arrives(f):
+        own_gather[f].arrive()
         to_sibling[f].start()
         pl.when(~apart)(across[f].start)
-        activate(1, f, True)
+
+    def away_arrives(f):
+        pl.when(apart)(halo[f].arrive)
+        pl.when(~apart)(across[f].wait_recv)
+        activate(away, f, inside)
+
+    sections = [ready(fin.at[0, f], fin.at[1, f], s_f.at[f], r_f.at[f], sibling) for f in range(4)]
+
+    def decode(pair, value):
+        for t in range(2):
+            f = pair * 2 + t
+            fin[0, f] = (resid[:, f * X : (f + 1) * X] + join(value, t)).astype(BF16)
+            pl.when(s == 1 - pair)(sections[f].start)
+
+    own_arrives(0)
+    own_arrives(1)
+    activate(1, 0, True)
+    activate(1, 1, True)
     loads[8].wait()
-    for pair in range(2):
-        total[pair, 0:288, 0 : 2 * X] = taps(w2, act2, 1, pair)
-    for f in range(4):
+    total[0, 0:288, :] = taps(w2, act2, 1, 0, 2)
+    for f in range(2):
         to_sibling[f].wait_recv()
         activate(near, f, True)
-    for pair in range(2):
-        total[pair, 0:288, 0 : 2 * X] += taps(w2, act2, near, pair)
-    inside = jnp.where(s == 0, b > 0, b < bands - 1)
-    finals = []
-    for pair in range(2):
-        for f in (2 * pair, 2 * pair + 1):
-
-            @pl.when(apart)
-            def _():
-                for copy in halo[f]:
-                    copy.wait_recv()
-
-            pl.when(~apart)(across[f].wait_recv)
-            activate(away, f, inside)
-        value = total[pair, 0:288, 0 : 2 * X] + taps(w2, act2, away, pair)
-        for t in range(2):
-            f = pair * 2 + t
-            decoded = (resid[:, f * X : (f + 1) * X] + join(value, t)).astype(BF16)
-            fin[0, f] = decoded
-    sections = remote(
-        fin.at[0, pl.ds(2 * (1 - s), 2)], fin.at[1, pl.ds(2 * (1 - s), 2)], s_f, r_f, sibling
-    )
-    sent.append(sections)
+    total[0, 0:288, :] += taps(w2, act2, near, 0, 2)
+    own_arrives(2)
+    own_arrives(3)
+    for f in range(2):
+        away_arrives(f)
+    decode(0, total[0, 0:288, :] + taps(w2, act2, away, 0, 2))
+    activate(1, 2, True)
+    activate(1, 3, True)
+    total[1, 0:288, :] = taps(w2, act2, 1, 2, 2)
+    for f in (2, 3):
+        to_sibling[f].wait_recv()
+        activate(near, f, True)
+    total[1, 0:288, :] += taps(w2, act2, near, 2, 2)
+    for f in (2, 3):
+        away_arrives(f)
+    decode(1, total[1, 0:288, :] + taps(w2, act2, away, 2, 2))
     for t in range(2):
         out_ref[t, s] = fin[0, 2 * s + t]
-    sections.wait_recv()
     for t in range(2):
+        for seg in range(2):
+            pl.when(s == seg)(sections[2 * seg + t].wait_recv)
         out_ref[t, 1 - s] = fin[1, 2 * s + t]
     for seg in range(2):
         pl.when(passes & (goal[0] == seg))(beyond[seg].wait_send)
-    for copy in sent + sum(own_gather, []) + to_sibling:
+    for f in range(4):
+        pl.when(s == 1 - f // 2)(sections[f].wait_send)
+    for copy in sent + to_sibling:
         copy.wait_send()
+    for gather in own_gather:
+        gather.sent()
 
     @pl.when(apart)
     def _():
-        for copy in sum(halo, []):
-            copy.wait_send()
+        for gather in halo:
+            gather.sent()
 
     @pl.when(~apart)
     def _():
@@ -365,7 +431,7 @@
     dma = pltpu.SemaphoreType.DMA
     out = pl.pallas_call(
         kernel,
-        out_shape=jax.ShapeDtypeStruct((2, 2, OWN, X), BF16),
+        out_shape=pltpu.VMEM((2, 2, OWN, X), BF16),
         in_specs=[hbm] * 9,
         out_specs=vmem,
         scratch_shapes=[
@@ -377,7 +443,9 @@
             pltpu.VMEM((1, OWN), F32),
             pltpu.VMEM((2592, C), BF16),
             pltpu.VMEM((2592, C), BF16),
-            pltpu.VMEM((4, 72, X), F32),
+            pltpu.VMEM((4, 64, X), BF16),
+            pltpu.VMEM((64, X), F32),
+            pltpu.VMEM((4, 8, X), F32),
             pltpu.VMEM((2, C, 256), BF16),
             pltpu.VMEM((512, OWN), BF16),
             pltpu.VMEM((5, 4, 32, X), BF16),
@@ -389,12 +457,12 @@
             pltpu.VMEM((2, C, X), F32),
             pltpu.VMEM((OWN, 4 * X), F32),
             pltpu.VMEM((2, 4, OWN, X), BF16),
-            dma((9,)), dma((3,)), dma((3,)), dma((3,)), dma((3,)), dma, dma, dma((6,)), dma((7,)),
-            dma((4, 3)), dma((4, 3)), dma((4,)), dma((4,)), dma((4, 3)), dma((4, 3)), dma((4,)), dma((4,)),
-            dma, dma,
+            dma((9,)), dma((6,)), dma((6,)), dma((3,)), dma((3,)), dma, dma, dma((6,)), dma((7,)),
+            dma((4, 4)), dma((4, 4)), dma((4,)), dma((4,)), dma((4, 4)), dma((4, 4)), dma((4,)), dma((4,)),
+            dma((4,)), dma((4,)),
         ],
         compiler_params=pltpu.CompilerParams(
-            collective_id=0, has_side_effects=True, vmem_limit_bytes=63 * 2**20
+            collective_id=0, has_side_effects=True, vmem_limit_bytes=60 * 10**6
         ),
     )(
         hidden_states.reshape(128, 1280),

time: 51.2 us -> 47.7 us (0.932)
  Pallas kernels: 49.5 us -> 46.8 us
  local copies, waits for them, and re-layouts: 1.61 us -> 0.72 us
    pallas_call x1, Pallas kernels: 49.5 us -> 46.8 us  [body(): pl.pallas_call(kernel, out_shape=pltpu.VMEM((2, 2, OWN, X), BF16), in_spe...]
    transpose x1, local copies, waits for them, and re-layouts: 1.61 us -> 0.72 us  [body(): return out.transpose(2, 0, 1, 3)]
where the time goes in v2:
time: 47.7 us; the launch traced here: 47.6 us
  Pallas kernels  46.8 us (98%)
  local copies, waits for them, and re-layouts  0.72 us (2%)
    pallas_call x1, Pallas kernels, body(): pl.pallas_call(kernel, out_shape=pltpu.VMEM((2, 2, OWN, X), BF16), in_spe...  46.8 us

profile of v2, /device:TPU:1, one launch (start us, length us, event | category | flops | bytes accessed | tf_op | source)
XLA Modules:
  0.0 47.6 jit_solution(5741709352815975900)
XLA Ops:
  0.0 46.8 %shard_map.91 = bf16[2,2,96,128]{3,2,1,0:T(8,128)(2,1)S(1)} custom-call(bf16[128,1280]{1,0:T(8,128)(2,1)} %bitcast.15, f32[10,128]{1,0:T(8,128)} %bitcast.18, f32[10,128]{1,0:T(8,128)} %bitcast.19, bf16[64,1280]{1,0:T(8,128)(2,1)} %bitcast.16, bf16[432,96]{1,0:T(8,128)(2,1)} %bitcast.17, bf16[2592,384]{1,0:T(8,128)(2,1)} %bitcast.13, f32[1,96]{1,0:T(1,128)} %bitcast.20, ...), custom_call_target="tpu_custom_call" | custom-call | tf_op jit(solution)/shard_map/pallas_call | solution.py:432
  46.8 0.7 %copy.10 = bf16[96,2,2,128]{3,2,1,0:T(2,128)(2,1)} copy(bf16[96,2,2,128]{3,0,2,1:T(8,128)(2,1)S(1)} %bitcast.12) | data formatting | bytes 196608 | tf_op jit(solution)/shard_map/transpose | solution.py:478

commit v3 on v2

--- a/solution.py
+++ b/solution.py
@@ -99,33 +99,33 @@
     raised = weight * (1.0 + lanes_of(scale_ref))
     high = raised.astype(BF16)
     low = (raised - high.astype(F32)).astype(BF16)
+    lift = jnp.sum(high.astype(F32) + low.astype(F32), axis=1, keepdims=True)
+    stats[c] = jnp.zeros((8, X), F32)
+    stats[c, 2:3, :] = as_row(lift)
+    stats[c, 3:4, :] = as_row(jnp.sum(weight * lanes_of(shift_ref), axis=1, keepdims=True))
     for load in loads[3:6]:
         load.wait()
+    stats[c, 4:5, 0:OWN] = g1_ref[...]
+    stats[c, 5:6, 0:OWN] = g2_ref[...]
     both = lax.dot_general(jnp.concatenate([high, low], axis=0), h_ref[...], NT, preferred_element_type=F32)
     states = h_ref[...].astype(F32)
     sums = as_row(jnp.sum(states, axis=1, keepdims=True))
-    lift = jnp.sum(high.astype(F32) + low.astype(F32), axis=1, keepdims=True)
+    stats[c, 0:1, :] = sums
+    stats[c, 1:2, :] = as_row(jnp.sum(states * states, axis=1, keepdims=True))
     exact[...] = both[0:64] + both[64:128] - lift * (sums / 1280)
     parts[c] = exact[...].astype(BF16)
-    stats[c] = jnp.zeros((8, X), F32)
-    stats[c, 0:1, :] = sums
-    stats[c, 1:2, :] = as_row(jnp.sum(states * states, axis=1, keepdims=True))
-    stats[c, 2:3, :] = as_row(lift)
-    stats[c, 3:4, :] = as_row(jnp.sum(weight * lanes_of(shift_ref), axis=1, keepdims=True))
-    stats[c, 4:5, 0:OWN] = g1_ref[...]
-    stats[c, 5:6, 0:OWN] = g2_ref[...]
 
     pl.semaphore_wait(barrier, 8 + passes.astype(jnp.int32))
     first = [remote(parts.at[c], parts.at[c], s_p.at[d], r_p.at[d], zpeers[d]) for d in (1, 0, 2)]
     first += [remote(stats.at[c], stats.at[c], s_p.at[3 + d], r_p.at[3 + d], zpeers[d]) for d in (1, 0, 2)]
-    sent += first
-
     own_rows = pl.ds(pl.multiple_of(c * OWN, OWN), OWN)
     loads[6].wait()
     ewp[432:512, :] = jnp.zeros((80, OWN), BF16)
     eye96 = (iota((OWN, OWN), 0) == iota((OWN, OWN), 1)).astype(F32).astype(BF16)
     half = ewp[pl.ds(pl.multiple_of(s * 256, 256), 256), :]
     ewg[s, own_rows, :] = lax.dot_general(eye96, half, NT, preferred_element_type=F32).astype(BF16)
+    for copy in first:
+        copy.wait_send()
     gather_e = [
         remote(ewg.at[s, own_rows], ewg.at[s, own_rows], s_e.at[d], r_e.at[d], zpeers[d]) for d in range(3)
     ]
@@ -307,14 +307,16 @@
             self.into[0].wait_recv()
             self.into[2].wait_recv()
 
+        def relayed(self):
+            if self.relay is not None:
+                pl.when(between)(self.relay.wait_send)
+
         def sent(self):
             for copy, when in zip(self.out, self.direct):
                 if when is None:
                     copy.wait_send()
                 else:
                     pl.when(when)(copy.wait_send)
-            if self.relay is not None:
-                pl.when(between)(self.relay.wait_send)
 
     own_gather = [Gather(f, 1, s_g, r_g) for f in range(4)]
     halo = [Gather(f, away, s_h, r_h) for f in range(4)]
@@ -393,6 +395,24 @@
         to_sibling[f].wait_recv()
         activate(near, f, True)
     total[1, 0:288, :] += taps(w2, act2, near, 2, 2)
+    for seg in range(2):
+        pl.when(passes & (goal[0] == seg))(beyond[seg].wait_send)
+    for copy in sent + to_sibling:
+        copy.wait_send()
+    for gather in own_gather:
+        gather.sent()
+        gather.relayed()
+
+    @pl.when(apart)
+    def _():
+        for gather in halo:
+            gather.sent()
+
+    @pl.when(~apart)
+    def _():
+        for copy in across:
+            copy.wait_send()
+
     for f in (2, 3):
         away_arrives(f)
     decode(1, total[1, 0:288, :] + taps(w2, act2, away, 2, 2))
@@ -402,24 +422,13 @@
         for seg in range(2):
             pl.when(s == seg)(sections[2 * seg + t].wait_recv)
         out_ref[t, 1 - s] = fin[1, 2 * s + t]
-    for seg in range(2):
-        pl.when(passes & (goal[0] == seg))(beyond[seg].wait_send)
     for f in range(4):
         pl.when(s == 1 - f // 2)(sections[f].wait_send)
-    for copy in sent + to_sibling:
-        copy.wait_send()
-    for gather in own_gather:
-        gather.sent()
 
     @pl.when(apart)
     def _():
         for gather in halo:
-            gather.sent()
-
-    @pl.when(~apart)
-    def _():
-        for copy in across:
-            copy.wait_send()
+            gather.relayed()
 
 
 def body(

time: 47.7 us -> 47.4 us (level)
  no operation moved by 1% of the time
where the time goes in v3:
time: 47.4 us; the launch traced here: 47.3 us
  Pallas kernels  46.6 us (98%)
  local copies, waits for them, and re-layouts  0.72 us (2%)
    pallas_call x1, Pallas kernels, body(): pl.pallas_call(kernel, out_shape=pltpu.VMEM((2, 2, OWN, X), BF16), in_spe...  46.6 us

profile of v3, /device:TPU:1, one launch (start us, length us, event | category | flops | bytes accessed | tf_op | source)
XLA Modules:
  0.0 47.3 jit_solution(15944011294370615298)
XLA Ops:
  0.0 46.6 %shard_map.91 = bf16[2,2,96,128]{3,2,1,0:T(8,128)(2,1)S(1)} custom-call(bf16[128,1280]{1,0:T(8,128)(2,1)} %bitcast.15, f32[10,128]{1,0:T(8,128)} %bitcast.18, f32[10,128]{1,0:T(8,128)} %bitcast.19, bf16[64,1280]{1,0:T(8,128)(2,1)} %bitcast.16, bf16[432,96]{1,0:T(8,128)(2,1)} %bitcast.17, bf16[2592,384]{1,0:T(8,128)(2,1)} %bitcast.13, f32[1,96]{1,0:T(1,128)} %bitcast.20, ...), custom_call_target="tpu_custom_call" | custom-call | tf_op jit(solution)/shard_map/pallas_call | solution.py:441
  46.6 0.7 %copy.10 = bf16[96,2,2,128]{3,2,1,0:T(2,128)(2,1)} copy(bf16[96,2,2,128]{3,0,2,1:T(8,128)(2,1)S(1)} %bitcast.12) | data formatting | bytes 196608 | tf_op jit(solution)/shard_map/transpose | solution.py:487
